TPU v7x, 32 devices: a whole 2x2x4 slice. The times are simulated.
32 devices in a mesh: groups: 2 (over x), expert: 2 (over core), blk: 8 (over z, y).
Axes of the slice: x: 2, y: 2, z: 4, core: 2. Of those that a mesh axis runs over, the one named last changes fastest.
Arguments:
- residual: bfloat16 [640, 6144], P(('groups', 'expert', 'blk')), parts along dimension 0, may hold values from -6 to 6
- queries: bfloat16 [640, 6144], P(('groups', 'expert', 'blk')), parts along dimension 0, may hold values from -6 to 6
- keys: bfloat16 [640, 32, 1024], P(('groups', 'expert', 'blk')), parts along dimension 0, may hold values from -6 to 6
- values: bfloat16 [640, 32, 1024], P(('groups', 'expert', 'blk')), parts along dimension 0, may hold values from -6 to 6
- lengths: int32 [640], P(('groups', 'expert', 'blk')), parts along dimension 0, may hold values from 2 to 32, as said below
- norm_gain: float32 [6144], replicated, may hold values from 0.5 to 1.5
- routes: int32 [640, 2], P(('groups', 'expert', 'blk')), parts along dimension 0, may hold values from 0 to 7, as said below
- gate_scores: float32 [640, 2], P(('groups', 'expert', 'blk')), parts along dimension 0, may hold values from 0.25 to 4
- w_gate: bfloat16 [2, 6144, 8192], P('expert', None, 'blk'), may hold values from -0.078125 to 0.078125
- w_up: bfloat16 [2, 6144, 8192], P('expert', None, 'blk'), may hold values from -0.078125 to 0.078125
- w_down: bfloat16 [2, 8192, 6144], P('expert', 'blk'), may hold values from -0.0625 to 0.0625
Outputs:
- mixed: bfloat16 [640, 6144], P(('groups', 'expert', 'blk')), parts along dimension 0
There are 2 independent parts, one for each index of `groups`. A program takes and returns all parts, laid end to end along the dimension named above; an argument that names none is the same for every part. Nothing has to cross between parts.
Inputs may be any that keep to these rules, and one draw needn't show every extreme that they name: `routes`: each request names two different experts. In the requests of one aligned block of 20, no expert is named by more than 6; one expert below 2 is named by exactly 6 in every block. `lengths`: some request has exactly 32 live positions.
All inputs are finite; a program needn't handle non-finite values.
Results may differ from a plain program's by a relative error of at most 0.005.
Values may be sent and summed in bfloat16 or wider, within the bound.
A program may use at most 128 MiB of HBM per device.

v0:
```python
import jax
import jax.numpy as jnp
from jax import lax
from jax.sharding import PartitionSpec as P

D = 6144
HEADS = 48
KV_HEADS = 8
HEAD_DIM = 128
CAP = 6


def on_device(
    residual, queries, keys, values, lengths, norm_gain, routes, gate_scores, w_gate, w_up, w_down
):
    row_count = residual.shape[0]
    cache_len = keys.shape[1]
    group_size = HEADS // KV_HEADS
    expert_count = lax.axis_size("expert")
    blk_count = lax.axis_size("blk")
    query_heads = queries.reshape(row_count, KV_HEADS, group_size, HEAD_DIM)
    key_heads = keys.reshape(row_count, cache_len, KV_HEADS, HEAD_DIM)
    value_heads = values.reshape(row_count, cache_len, KV_HEADS, HEAD_DIM)
    scores = jnp.einsum(
        "rgjd,rtgd->rgjt", query_heads, key_heads, preferred_element_type=jnp.float32
    ) * HEAD_DIM ** (-0.5)
    position = jnp.arange(cache_len, dtype=jnp.int32)
    valid_mask = position[None, :] < lengths[:, None]
    scores = jnp.where(valid_mask[:, None, None, :], scores, jnp.float32(-1e30))
    top_score = jnp.max(scores, axis=-1, keepdims=True)
    exponent = jnp.exp(scores - top_score)
    attn_probs = (exponent / jnp.sum(exponent, axis=-1, keepdims=True)).astype(jnp.bfloat16)
    attended = jnp.einsum(
        "rgjt,rtgd->rgjd", attn_probs, value_heads, preferred_element_type=jnp.float32
    ).reshape(row_count, D)
    hidden_state = residual.astype(jnp.float32) + attended
    mean_square = jnp.mean(hidden_state * hidden_state, axis=1, keepdims=True)
    normed_rows = (hidden_state * lax.rsqrt(mean_square + 1e-05) * norm_gain[None, :]).astype(
        jnp.bfloat16
    )
    chosen = routes[:, :, None] == jnp.arange(expert_count, dtype=jnp.int32)[None, None, :]
    membership = jnp.sum(chosen.astype(jnp.int32), axis=1)
    gate_weights = gate_scores / jnp.sum(gate_scores, axis=1, keepdims=True)
    expert_weight = jnp.sum(gate_weights[:, :, None] * chosen.astype(jnp.float32), axis=1)
    earlier = jnp.cumsum(membership, axis=0) - membership
    slot_match = (earlier[:, :, None] == jnp.arange(CAP, dtype=jnp.int32)[None, None, :]) & (
        membership[:, :, None] > 0
    )
    dispatch_table = jnp.transpose(slot_match, (1, 2, 0)).astype(jnp.bfloat16)
    send_rows = jnp.einsum(
        "ecr,rd->ecd", dispatch_table, normed_rows, preferred_element_type=jnp.float32
    ).astype(jnp.bfloat16)
    combine_table = expert_weight[:, :, None] * slot_match.astype(jnp.float32)
    gate_local = w_gate[0]
    up_local = w_up[0]
    down_local = w_down[0]
    unit_count = gate_local.shape[1]
    arrived = lax.all_to_all(send_rows, "expert", split_axis=0, concat_axis=0, tiled=True)
    piece = lax.all_gather(arrived, "blk", axis=0, tiled=True)
    flat_rows = piece.reshape(-1, D)
    gate_part = jnp.dot(flat_rows, gate_local, preferred_element_type=jnp.float32)
    up_part = jnp.dot(flat_rows, up_local, preferred_element_type=jnp.float32)
    activated = (jax.nn.silu(gate_part) * up_part).astype(jnp.bfloat16)
    gathered = activated.reshape(piece.shape[0], CAP, unit_count)
    by_owner = jnp.transpose(
        gathered.reshape(blk_count, expert_count, CAP, unit_count), (1, 0, 2, 3)
    )
    ordered = jnp.transpose(by_owner, (1, 0, 2, 3)).reshape(-1, unit_count)
    product = jnp.dot(ordered, down_local, preferred_element_type=jnp.float32).astype(jnp.bfloat16)
    summed = lax.psum_scatter(
        lax.optimization_barrier(product).astype(jnp.float32).astype(jnp.bfloat16),
        "blk",
        scatter_dimension=0,
        tiled=True,
    )
    outputs = summed.reshape(expert_count, CAP, D)
    returned = lax.all_to_all(outputs, "expert", split_axis=0, concat_axis=0, tiled=True)
    weighted = jnp.einsum(
        "rec,ecd->rd", combine_table, returned.astype(jnp.float32), precision=lax.Precision.HIGHEST
    )
    return (hidden_state + weighted).astype(jnp.bfloat16)


def solution(mesh):
    return jax.shard_map(
        on_device,
        mesh=mesh,
        in_specs=(
            P(("groups", "expert", "blk"), None),
            P(("groups", "expert", "blk"), None),
            P(("groups", "expert", "blk"), None, None),
            P(("groups", "expert", "blk"), None, None),
            P(("groups", "expert", "blk")),
            P(),
            P(("groups", "expert", "blk"), None),
            P(("groups", "expert", "blk"), None),
            P("expert", None, "blk"),
            P("expert", None, "blk"),
            P("expert", "blk", None),
        ),
        out_specs=P(("groups", "expert", "blk"), None),
        check_vma=False,
    )
```

profile of v0, /device:TPU:1, one launch (start us, length us, event | category | flops | bytes accessed | tf_op | source)
XLA Modules:
  0.0 152.7 jit_solution(2878978509694546401)
XLA Ops:
  6.5 0.0 copy-start
  6.5 0.0 all-gather.2.cloned.1.call-start
  6.5 0.8 convert_reduce_fusion
  7.3 0.1 copy.38
  7.4 0.7 iota_compare_fusion
  8.2 0.1 copy.41
  8.3 1.3 reshape.63
  9.6 2.1 %fusion.24 = f32[20,8,6,32]{3,2,1,0:T(8,128)S(1)} fusion(bf16[20,8,6,128]{3,2,1,0:T(8,128)(2,1)S(1)} %reshape.63, pred[20,32]{1,0:T(8,128)(4,1)S(1)} %iota_compare_fusion, bf16[20,32,1024]{2,1,0:T(8,128)(2,1)} %param.13), kind=kOutput, calls=%fused_computation.21 | convolution fusion | flops 7925760 | bytes 1680000 | tf_op jit(solution)/shard_map/rgjd,rtgd->rgjt/dot_general | solution.py:24
  11.7 0.4 fusion.59
  12.2 0.0 copy-done
  12.2 3.2 %fusion.14 = f32[20,8,6,128]{3,2,1,0:T(8,128)} fusion(f32[20,8,6]{2,1,0:T(8,128)S(1)} %fusion.59, f32[20,8,6,32]{3,2,1,0:T(8,128)S(1)} %fusion.24, bf16[20,32,1024]{2,1,0:T(8,128)(2,1)S(1)} %copy-done), kind=kOutput, calls=%fused_computation.13 | convolution fusion | flops 7957471 | bytes 1928960 | tf_op jit(solution)/shard_map/rgjt,rtgd->rgjd/dot_general | solution.py:33
  15.4 0.0 copy-start.1
  15.4 0.0 copy-start.2
  15.4 1.3 reshape.66
  16.6 0.0 copy-done.1
  16.6 0.0 copy-start.4
  16.6 0.2 multiply_reduce_fusion
  16.9 0.0 copy-done.2
  16.9 0.3 convolution_convert_fusion
  17.2 4.3 %all_to_all.10 = bf16[2,6,6144]{2,1,0:T(8,128)(2,1)} all-to-all(bf16[2,6,6144]{2,1,0:T(8,128)(2,1)S(1)} %convolution_convert_fusion), channel_id=1, replica_groups=mesh['groups'=2,'expert'=2,'blk'=8] {'expert'}, dimensions={0} | all-to-all | bytes 294912 | tf_op jit(solution)/shard_map/all_to_all | solution.py:58
  21.5 0.0 all-gather.2.cloned.1.call-update
  21.5 0.0 copy-done.4
  21.5 46.1 %all-gather.2.cloned.1.call-done = bf16[16,6,6144]{2,1,0:T(8,128)(2,1)} async-done(((bf16[2,6,6144]{2,1,0:T(8,128)(2,1)}), bf16[16,6,6144]{2,1,0:T(8,128)(2,1)}) %all-gather.2.cloned.1.call-update) | async-done | bytes 1179664 | tf_op jit(solution)/shard_map/all_gather | solution.py:59
  67.6 1.6 %reshape.67 = bf16[96,6144]{1,0:T(8,128)(2,1)S(1)} reshape(bf16[16,6,6144]{2,1,0:T(8,128)(2,1)} %all-gather.2.cloned.1.call-done) | data formatting | bytes 2359296 | tf_op jit(solution)/shard_map/reshape | solution.py:60
  69.2 7.5 %fusion.6 = f32[96,1024]{1,0:T(8,128)} fusion(bf16[96,6144]{1,0:T(8,128)(2,1)S(1)} %reshape.67, bf16[1,6144,1024]{2,1,0:T(8,128)(2,1)} %param.19), kind=kOutput, calls=%fused_computation.5 | convolution fusion | flops 1207959552 | bytes 14155776 | tf_op jit(solution)/shard_map/dot_general | solution.py:61
  76.6 13.5 %fusion.8 = bf16[96,6144]{1,0:T(8,128)(2,1)} fusion(bf16[1,1024,6144]{2,1,0:T(8,128)(2,1)} %param.21, bf16[96,6144]{1,0:T(8,128)(2,1)S(1)} %reshape.67, bf16[1,6144,1024]{2,1,0:T(8,128)(2,1)} %param.20, f32[96,1024]{1,0:T(8,128)} %fusion.6), kind=kOutput, calls=%fused_computation.7 | convolution fusion | flops 2417098752 | bytes 27918336 | tf_op jit(solution)/shard_map/dot_general | solution.py:69
  90.1 0.0 copy-start.5
  90.1 0.0 copy-start.3
  90.1 36.1 %fusion = bf16[16,6144]{1,0:T(8,128)(2,1)S(1)} fusion(bf16[96,6144]{1,0:T(8,128)(2,1)} %fusion.8), kind=kCustom, calls=%all-reduce-scatter | all-reduce-scatter fusion | flops 786433 | bytes 1376768
  126.2 3.7 %collective-permute-start = (bf16[16,6144]{1,0:T(8,128)(2,1)S(1)}, bf16[16,6144]{1,0:T(8,128)(2,1)S(1)}, u32[]{:S(2)}, u32[]{:S(2)}) collective-permute-start(bf16[16,6144]{1,0:T(8,128)(2,1)S(1)} %fusion), channel_id=1, source_target_pairs={{0,1},{1,2},{2,3},{3,4},{4,5},{5,6},{6,7},{8,9},{9,10},{10,11},{11... | collective-permute-start | bytes 589832
  130.0 1.3 collective-permute-start.1
  131.3 0.1 copy.40
  131.4 0.0 copy-done.5
  131.4 0.6 dynamic-slice.4
  132.6 0.0 copy-done.3
  132.7 1.2 collective-permute-done.1
  133.9 0.0 collective-permute-done
  133.9 1.1 concatenate
  135.0 0.1 constant_dynamic-slice_fusion
  135.1 0.1 reshape.68
  135.1 9.5 %all_to_all.11 = bf16[2,6,6144]{2,1,0:T(8,128)(2,1)S(1)} all-to-all(bf16[2,6,6144]{2,1,0:T(8,128)(2,1)S(1)} %reshape.68), channel_id=1, replica_groups=mesh['groups'=2,'expert'=2,'blk'=8] {'expert'}, dimensions={0} | all-to-all | bytes 294912 | tf_op jit(solution)/shard_map/all_to_all | solution.py:77
  144.6 1.2 fusion.12
  (9 shorter events, 0.2 us)
Async XLA Ops:
  6.5 5.6 %copy-start = (bf16[20,32,1024]{2,1,0:T(8,128)(2,1)S(1)}, bf16[20,32,1024]{2,1,0:T(8,128)(2,1)}, u32[]{:S(2)}) copy-start(bf16[20,32,1024]{2,1,0:T(8,128)(2,1)} %param.14) | copy-start | bytes 3932164
  6.5 61.0 %all-gather.2.cloned.1.call-start = ((), (), s32[]{:S(2)}) async-start(), calls=%async_computation.2 | async-start | bytes 1769472 | tf_op jit(solution)/shard_map/all_gather | solution.py:59
  15.4 1.3 copy-start.1
  15.4 1.5 copy-start.2
  16.6 4.8 %copy-start.4 = (f32[20,2]{0,1:T(2,128)S(1)}, f32[20,2]{0,1:T(2,128)}, u32[]{:S(2)}) copy-start(f32[20,2]{0,1:T(2,128)} %param.18) | copy-start | bytes 484
  90.1 41.3 %copy-start.5 = (u32[32]{0:T(128)S(1)}, u32[32]{0:T(128)}, u32[]{:S(2)}) copy-start(u32[32]{0:T(128)} %constant.36) | copy-start | bytes 388
  90.1 42.5 %copy-start.3 = (s32[20,2]{0,1:T(2,128)S(1)}, s32[20,2]{0,1:T(2,128)}, u32[]{:S(2)}) copy-start(s32[20,2]{0,1:T(2,128)} %param.17) | copy-start | bytes 484
  126.2 7.6 %collective-permute-start = (bf16[16,6144]{1,0:T(8,128)(2,1)S(1)}, bf16[16,6144]{1,0:T(8,128)(2,1)S(1)}, u32[]{:S(2)}, u32[]{:S(2)}) collective-permute-start(bf16[16,6144]{1,0:T(8,128)(2,1)S(1)} %fusion), channel_id=1, source_target_pairs={{0,1},{1,2},{2,3},{3,4},{4,5},{5,6},{6,7},{8,9},{9,10},{10,11},{11... | collective-permute-start | bytes 589832
  130.0 3.9 %collective-permute-start.1 = (bf16[12,6144]{1,0:T(8,128)(2,1)S(1)}, bf16[12,6144]{1,0:T(8,128)(2,1)S(1)}, u32[]{:S(2)}, u32[]{:S(2)}) collective-permute-start(bf16[12,6144]{1,0:T(8,128)(2,1)S(1)} %slice), channel_id=1, source_target_pairs={{0,2},{1,3},{2,4},{3,5},{4,6},{5,7},{8,10},{9,11},{10,12},{11,13},... | collective-permute-start | bytes 442376
Sparse Core Ops, SparseCore 0:
  21.6 45.9 all-gather.1
where the time goes:
time: 153 us
  blocking collectives  49.9 us (33%)
  waiting for transfers between devices  47.3 us (31%)
  matrix products  27.7 us (18%)
  between operations  14.2 us (9%)
  local copies, waits for them, and re-layouts  6.29 us (4%)
  starting transfers between devices  5.05 us (3%)
  other arithmetic  2.28 us (1%)
    all_gather x1, waiting for transfers between devices, on_device(): piece = lax.all_gather(arrived, 'blk', axis=0, tiled=True)  46.1 us
    unnamed x1, blocking collectives  36.1 us
    dot_general x1, matrix products, on_device(): jnp.dot(ordered, down_local, preferred_element_type=jnp.float32)  13.5 us
    all_to_all x1, blocking collectives, on_device(): lax.all_to_all(outputs, 'expert', split_axis=0, concat_axis=0, tiled=True)  9.52 us
    dot_general x1, matrix products, on_device(): jnp.dot(flat_rows, gate_local, preferred_element_type=jnp.float32)  7.46 us
    unnamed x2, starting transfers between devices  5.04 us
    all_to_all x1, blocking collectives, on_device(): lax.all_to_all(send_rows, 'expert', split_axis=0, concat_axis=0, tiled=True)  4.29 us
    dot_general x1, matrix products, on_device(): jnp.einsum('rgjt,rtgd->rgjd', attn_probs, value_heads, preferred_element_...  3.19 us
  transfers between devices with their start and end apart: 3, of which 2 were waited for; matrix products, arithmetic and copies ran while one was open for 0% of the time, Pallas kernels for 0%

commit v1 on v0

v1 whole, which is shorter than its diff:
```python
import functools

import jax
import jax.numpy as jnp
from jax import lax
from jax.experimental import pallas as pl
from jax.experimental.pallas import tpu as pltpu
from jax.sharding import PartitionSpec as P

HEADS = 48
KV_HEADS = 8
HEAD_DIM = 128
GROUP = HEADS // KV_HEADS
CAP = 6
PIECE = 16
LIVE = 2 * CAP
CHUNK = 1024
QUARTER = CHUNK // 4
PACK = 3 * QUARTER
PAD = 24
TILE = 128
MESH = pl.DeviceIdType.MESH


def f32_dot(a, b):
    return jnp.dot(a, b, preferred_element_type=jnp.float32)


def kernel(
    n, residual, queries, meta, gain, keys, values, w_gate, w_up, w_down, mixed,
    kbuf, vbuf, wg, wu, wd, qs, hid, live,
    osend, inbox, gath, xfull, gacc, uacc, act,
    part, ybuf, red, zbuf, fin, pfin,
    kv_sem, wg_sem, wu_sem, wd_sem,
    i_sems, z_sems, y_sems, ry_sems, rz_sems, ri_sems,
):
    rows = residual.shape[0]
    width = residual.shape[1]
    cache_len = keys.shape[1]
    chunks = width // CHUNK
    units = wg.shape[1]
    unit_tile = min(units, QUARTER)
    nc = n // 2
    total = n * PIECE
    core = lax.axis_index("expert")
    me = lax.axis_index("blk")
    yc = lax.rem(me, 2)
    zc = lax.div(me, 2)
    other = 1 - core
    y_partner = me + 1 - 2 * yc

    def column_peer(k):
        return lax.rem(zc + k, nc) * 2 + yc

    barrier = pltpu.get_barrier_semaphore()
    pl.semaphore_signal(barrier, inc=1, device_id={"expert": other}, device_id_type=MESH)
    pl.semaphore_signal(barrier, inc=1, device_id={"blk": y_partner}, device_id_type=MESH)
    for k in range(1, nc):
        pl.semaphore_signal(barrier, inc=1, device_id={"blk": column_peer(k)}, device_id_type=MESH)

    key_copy = pltpu.make_async_copy(keys, kbuf, kv_sem.at[0])
    value_copy = pltpu.make_async_copy(values, vbuf, kv_sem.at[1])
    key_copy.start()
    value_copy.start()

    def chunk_at(c):
        return pl.ds(pl.multiple_of(c * CHUNK, CHUNK), CHUNK)

    def gate_copy(c):
        return pltpu.make_async_copy(w_gate.at[0, chunk_at(c)], wg.at[chunk_at(c)], wg_sem.at[c])

    def up_copy(c):
        return pltpu.make_async_copy(w_up.at[0, chunk_at(c)], wu.at[chunk_at(c)], wu_sem.at[c])

    def down_copy(c):
        return pltpu.make_async_copy(w_down.at[0, :, chunk_at(c)], wd.at[c], wd_sem.at[c])

    @pl.loop(0, chunks)
    def _(c):
        gate_copy(c).start()
        up_copy(c).start()

    @pl.loop(0, chunks)
    def _(c):
        down_copy(c).start()

    row_id = lax.broadcasted_iota(jnp.int32, (PAD, TILE), 0)
    lane_id = lax.broadcasted_iota(jnp.int32, (PAD, TILE), 1)

    def as_column(row):
        return jnp.sum(jnp.where(row_id == lane_id, row, 0.0), axis=1, keepdims=True)

    first, second = meta[0:1, :], meta[1:2, :]
    score0, score1 = meta[2:3, :], meta[3:4, :]
    lengths = as_column(meta[4:5, :])
    slot_row = lax.broadcasted_iota(jnp.int32, (PIECE, TILE), 0).astype(jnp.float32)
    slot_lane = lax.broadcasted_iota(jnp.int32, (PAD, PIECE), 1).astype(jnp.float32)
    base = (core * CAP).astype(jnp.float32)

    def tables(expert):
        wanted = expert.astype(jnp.float32)
        in_first, in_second = first == wanted, second == wanted
        member = jnp.where(in_first, 1.0, 0.0) + jnp.where(in_second, 1.0, 0.0)
        gate = (jnp.where(in_first, score0, 0.0) + jnp.where(in_second, score1, 0.0)) / (
            score0 + score1
        )
        member_column = as_column(member)
        earlier = jnp.sum(jnp.where(row_id < lane_id, member_column, 0.0), axis=0, keepdims=True)
        slot = jnp.where(member > 0, earlier + base, -100.0)
        slot_column = as_column(slot)
        send = [jnp.where((slot_row == slot) & (slot_row < LIVE), 1.0, 0.0)]
        take = [jnp.where((slot_lane == slot_column) & (slot_lane < LIVE), 1.0, 0.0)]
        for i in range(3):
            send.append(
                jnp.where((slot_row + (4 * i - LIVE) == slot) & (slot_row >= LIVE), 1.0, 0.0)
            )
            take.append(
                jnp.where(
                    (slot_lane + (4 * i - LIVE) == slot_column) & (slot_lane >= LIVE), 1.0, 0.0
                )
            )
        return (
            [s[:, :PAD] for s in send],
            [t.astype(jnp.bfloat16) for t in take],
            as_column(gate),
        )

    send_own, take_own, gate_own = tables(core)
    send_other, take_other, gate_other = tables(other)
    send_main = jnp.concatenate([send_own[0], send_other[0]], axis=0).astype(jnp.bfloat16)
    send_tail = jnp.concatenate(
        [t for i in range(1, 4) for t in (send_own[i], send_other[i])], axis=0
    ).astype(jnp.bfloat16)

    place = lax.broadcasted_iota(jnp.int32, live.shape, 1) - cache_len * lax.broadcasted_iota(
        jnp.int32, live.shape, 0
    )
    place = place.astype(jnp.float32)
    live[...] = jnp.where((place >= 0) & (place < lengths), 1.0, 0.0)
    tail = (PAD - 16, width)
    qs[16:PAD, :] = jnp.zeros(tail, jnp.float32)
    hid[16:PAD, :] = jnp.zeros(tail, jnp.float32)
    qs[0:rows, :] = queries[...].astype(jnp.float32)
    hid[0:rows, :] = residual[...].astype(jnp.float32)
    key_copy.wait()
    value_copy.wait()

    def head(g, squares):
        def cols(j):
            return pl.ds(pl.multiple_of((g * GROUP + j) * HEAD_DIM, HEAD_DIM), HEAD_DIM)

        kv_cols = pl.ds(pl.multiple_of(g * HEAD_DIM, HEAD_DIM), HEAD_DIM)
        q = jnp.concatenate([qs[:, cols(j)] for j in range(GROUP)], axis=0).astype(jnp.bfloat16)
        k = kbuf[:, :, kv_cols].reshape(rows * cache_len, HEAD_DIM)
        v = vbuf[:, :, kv_cols].reshape(rows * cache_len, HEAD_DIM)
        scores = lax.dot_general(
            q, k, (((1,), (1,)), ((), ())), preferred_element_type=jnp.float32
        ) * HEAD_DIM ** (-0.5)
        scores = scores.reshape(GROUP, PAD, rows * cache_len)
        scores = jnp.where(live[...][None] > 0, scores, -1e30)
        exponent = jnp.exp(scores - jnp.max(scores, axis=-1, keepdims=True))
        probs = exponent / jnp.sum(exponent, axis=-1, keepdims=True)
        probs = probs.reshape(GROUP * PAD, rows * cache_len).astype(jnp.bfloat16)
        attended = f32_dot(probs, v)
        for j in range(GROUP):
            h = hid[:, cols(j)] + attended[j * PAD:(j + 1) * PAD]
            hid[:, cols(j)] = h
            squares = squares + h * h
        return squares

    squares = lax.fori_loop(0, KV_HEADS, head, jnp.zeros((PAD, HEAD_DIM), jnp.float32))
    inverse = lax.rsqrt(jnp.sum(squares, axis=1, keepdims=True) * (1.0 / width) + 1e-5)

    def in_chip(c):
        return pltpu.make_async_remote_copy(
            osend.at[c], inbox.at[c], i_sems.at[0, c], i_sems.at[1, c],
            device_id={"expert": other}, device_id_type=MESH,
        )

    def along_column(c, k):
        mine = gath.at[c, yc, zc]
        return pltpu.make_async_remote_copy(
            mine, mine, z_sems.at[0, c, k - 1], z_sems.at[1, c, k - 1],
            device_id={"blk": column_peer(k)}, device_id_type=MESH,
        )

    def from_column(c, k):
        theirs = gath.at[c, yc, lax.rem(zc + nc - k, nc)]
        return pltpu.make_async_remote_copy(
            theirs, theirs, z_sems.at[0, c, k - 1], z_sems.at[1, c, k - 1],
            device_id={"blk": column_peer(k)}, device_id_type=MESH,
        )

    def to_partner(c, y):
        column = gath.at[c, y]
        return pltpu.make_async_remote_copy(
            column, column, y_sems.at[0, c], y_sems.at[1, c],
            device_id={"blk": y_partner}, device_id_type=MESH,
        )

    pl.semaphore_wait(barrier, nc + 1)

    @pl.loop(0, chunks)
    def _(c):
        at = chunk_at(c)
        normed = (hid[:, at] * inverse * gain[:, at]).astype(jnp.bfloat16)
        main = f32_dot(send_main, normed[:, :PACK])
        last = f32_dot(send_tail, normed[:, PACK:])
        both = 2 * PIECE
        packed = main + jnp.concatenate([last[i * both:(i + 1) * both] for i in range(3)], axis=1)
        packed = packed.astype(jnp.bfloat16)
        gath[c, yc, zc] = packed[:PIECE]
        osend[c] = packed[PIECE:]
        in_chip(c).start()

    @pl.loop(0, chunks)
    def _(c):
        in_chip(c).wait_recv()
        gath[c, yc, zc] = (
            gath[c, yc, zc].astype(jnp.float32) + inbox[c].astype(jnp.float32)
        ).astype(jnp.bfloat16)
        for k in range(1, nc):
            along_column(c, k).start()

    span_a = lax.broadcasted_iota(jnp.int32, (TILE, TILE), 0)
    span_b = lax.broadcasted_iota(jnp.int32, (TILE, TILE), 1)
    in_piece = span_a & (PIECE - 1)
    spread, collect = [], []
    for i in range(3):
        spread.append(
            jnp.where(
                (span_b == span_a + (LIVE - 4 * i)) & (in_piece >= 4 * i) & (in_piece < 4 * i + 4),
                1.0, 0.0,
            )
        )
        collect.append(
            jnp.where((span_b == span_a - (LIVE - 4 * i)) & (in_piece >= LIVE), 1.0, 0.0)
        )
    spread = jnp.concatenate(spread, axis=1).astype(jnp.bfloat16)
    collect = jnp.concatenate(collect, axis=0).astype(jnp.bfloat16)
    groups = [slice(t, t + TILE) for t in range(0, total, TILE)]

    gacc[...] = jnp.zeros(gacc.shape, jnp.float32)
    uacc[...] = jnp.zeros(uacc.shape, jnp.float32)

    @pl.loop(0, chunks + 1)
    def _(s):
        @pl.when(s < chunks)
        def _():
            for k in range(1, nc):
                from_column(s, k).wait_recv()
            to_partner(s, yc).start()

        @pl.when(s > 0)
        def _():
            c = s - 1
            to_partner(c, 1 - yc).wait_recv()
            packed = gath[c].reshape(total, PACK)
            xfull[:, :PACK] = packed
            for group in groups:
                stacked = jnp.concatenate(
                    [packed[group, i * QUARTER:(i + 1) * QUARTER] for i in range(3)], axis=0
                )
                xfull[group, PACK:] = f32_dot(spread, stacked).astype(jnp.bfloat16)
            gate_copy(c).wait()
            up_copy(c).wait()

            @pl.loop(0, units // unit_tile)
            def _(t):
                tile = pl.ds(pl.multiple_of(t * unit_tile, unit_tile), unit_tile)
                x = xfull[...]
                gacc[:, tile] += f32_dot(x, wg[chunk_at(c), tile])
                uacc[:, tile] += f32_dot(x, wu[chunk_at(c), tile])

    @pl.loop(0, units // unit_tile)
    def _(t):
        tile = pl.ds(pl.multiple_of(t * unit_tile, unit_tile), unit_tile)
        g = gacc[:, tile]
        act[:, tile] = (g / (1.0 + jnp.exp(-g)) * uacc[:, tile]).astype(jnp.bfloat16)

    def sum_partner(c):
        return pltpu.make_async_remote_copy(
            part.at[c, 1 - yc], ybuf.at[c], ry_sems.at[0, c], ry_sems.at[1, c],
            device_id={"blk": y_partner}, device_id_type=MESH,
        )

    def sum_column(c, k):
        return pltpu.make_async_remote_copy(
            red.at[c, lax.rem(zc + k, nc)], zbuf.at[c, k - 1],
            rz_sems.at[0, c, k - 1], rz_sems.at[1, c, k - 1],
            device_id={"blk": column_peer(k)}, device_id_type=MESH,
        )

    def swap(c):
        return pltpu.make_async_remote_copy(
            fin.at[c], pfin.at[c], ri_sems.at[0, c], ri_sems.at[1, c],
            device_id={"expert": other}, device_id_type=MESH,
        )

    live_row = (lax.broadcasted_iota(jnp.int32, (total, QUARTER), 0) & (PIECE - 1)) < LIVE

    @pl.loop(0, chunks + 3)
    def _(s):
        @pl.when(s < chunks)
        def _():
            down_copy(s).wait()
            a = act[...]
            last = f32_dot(a, wd[s, :, PACK:]).astype(jnp.bfloat16)
            moved = [f32_dot(collect, last[group]) for group in groups]
            for i in range(3):
                y = f32_dot(a, wd[s, :, i * QUARTER:(i + 1) * QUARTER])
                extra = jnp.concatenate([m[i * TILE:(i + 1) * TILE] for m in moved], axis=0)
                packed = jnp.where(live_row, y, extra).astype(jnp.bfloat16)
                part[s, :, :, :, i * QUARTER:(i + 1) * QUARTER] = packed.reshape(
                    2, nc, PIECE, QUARTER
                )
            sum_partner(s).start()

        @pl.when((s >= 1) & (s <= chunks))
        def _():
            c = s - 1
            sum_partner(c).wait_recv()
            red[c] = (
                part[c, yc].astype(jnp.float32) + ybuf[c].astype(jnp.float32)
            ).astype(jnp.bfloat16)
            for k in range(1, nc):
                sum_column(c, k).start()

        @pl.when((s >= 2) & (s <= chunks + 1))
        def _():
            c = s - 2
            for k in range(1, nc):
                sum_column(c, k).wait_recv()
            value = red[c, zc].astype(jnp.float32)
            for k in range(1, nc):
                value = value + zbuf[c, k - 1].astype(jnp.float32)
            fin[c] = value.astype(jnp.bfloat16)
            swap(c).start()

        @pl.when(s >= 3)
        def _():
            c = s - 3
            swap(c).wait_recv()
            main = hid[:, pl.ds(pl.multiple_of(c * CHUNK, CHUNK), PACK)]
            last = hid[:, pl.ds(pl.multiple_of(c * CHUNK + PACK, QUARTER), QUARTER)]
            for take, gate, outs in (
                (take_own, gate_own, fin[c]), (take_other, gate_other, pfin[c])
            ):
                main = main + gate * f32_dot(take[0], outs)
                picked = f32_dot(take[1], outs[:, :QUARTER])
                for i in range(1, 3):
                    picked = picked + f32_dot(
                        take[i + 1], outs[:, i * QUARTER:(i + 1) * QUARTER]
                    )
                last = last + gate * picked
            mixed[:, pl.ds(pl.multiple_of(c * CHUNK, CHUNK), PACK)] = main[:rows].astype(
                jnp.bfloat16
            )
            mixed[:, pl.ds(pl.multiple_of(c * CHUNK + PACK, QUARTER), QUARTER)] = last[
                :rows
            ].astype(jnp.bfloat16)

    @pl.loop(0, chunks)
    def _(c):
        in_chip(c).wait_send()
        to_partner(c, yc).wait_send()
        sum_partner(c).wait_send()
        swap(c).wait_send()
        for k in range(1, nc):
            along_column(c, k).wait_send()
            sum_column(c, k).wait_send()


def on_device(
    residual, queries, keys, values, lengths, norm_gain, routes, gate_scores, w_gate, w_up, w_down
):
    n = lax.axis_size("blk")
    nc = n // 2
    rows, width = residual.shape
    cache_len = keys.shape[1]
    units = w_gate.shape[2]
    chunks = width // CHUNK
    total = n * PIECE
    meta = jnp.pad(
        jnp.concatenate(
            [routes.T.astype(jnp.float32), gate_scores.T, lengths[None].astype(jnp.float32)], axis=0
        ),
        ((0, 3), (0, TILE - rows)),
        constant_values=-1.0,
    )
    bf16, f32 = jnp.bfloat16, jnp.float32
    vmem = pl.BlockSpec(memory_space=pltpu.VMEM)
    anywhere = pl.BlockSpec(memory_space=pl.ANY)
    dma = pltpu.SemaphoreType.DMA
    return pl.pallas_call(
        functools.partial(kernel, n),
        out_shape=jax.ShapeDtypeStruct((rows, width), bf16),
        in_specs=[vmem] * 4 + [anywhere] * 5,
        out_specs=vmem,
        scratch_shapes=[
            pltpu.VMEM(keys.shape, bf16),
            pltpu.VMEM(values.shape, bf16),
            pltpu.VMEM((width, units), bf16),
            pltpu.VMEM((width, units), bf16),
            pltpu.VMEM((chunks, units, CHUNK), bf16),
            pltpu.VMEM((PAD, width), f32),
            pltpu.VMEM((PAD, width), f32),
            pltpu.VMEM((PAD, rows * cache_len), f32),
            pltpu.VMEM((chunks, PIECE, PACK), bf16),
            pltpu.VMEM((chunks, PIECE, PACK), bf16),
            pltpu.VMEM((chunks, 2, nc, PIECE, PACK), bf16),
            pltpu.VMEM((total, CHUNK), bf16),
            pltpu.VMEM((total, units), f32),
            pltpu.VMEM((total, units), f32),
            pltpu.VMEM((total, units), bf16),
            pltpu.VMEM((chunks, 2, nc, PIECE, PACK), bf16),
            pltpu.VMEM((chunks, nc, PIECE, PACK), bf16),
            pltpu.VMEM((chunks, nc, PIECE, PACK), bf16),
            pltpu.VMEM((chunks, nc - 1, PIECE, PACK), bf16),
            pltpu.VMEM((chunks, PIECE, PACK), bf16),
            pltpu.VMEM((chunks, PIECE, PACK), bf16),
            dma((2,)),
            dma((chunks,)),
            dma((chunks,)),
            dma((chunks,)),
            dma((2, chunks)),
            dma((2, chunks, nc - 1)),
            dma((2, chunks)),
            dma((2, chunks)),
            dma((2, chunks, nc - 1)),
            dma((2, chunks)),
        ],
        compiler_params=pltpu.CompilerParams(
            collective_id=0, has_side_effects=True, vmem_limit_bytes=60 * 1024 * 1024
        ),
    )(residual, queries, meta, norm_gain.reshape(1, width), keys, values, w_gate, w_up, w_down)


def solution(mesh):
    return jax.shard_map(
        on_device,
        mesh=mesh,
        in_specs=(
            P(("groups", "expert", "blk"), None),
            P(("groups", "expert", "blk"), None),
            P(("groups", "expert", "blk"), None, None),
            P(("groups", "expert", "blk"), None, None),
            P(("groups", "expert", "blk")),
            P(),
            P(("groups", "expert", "blk"), None),
            P(("groups", "expert", "blk"), None),
            P("expert", None, "blk"),
            P("expert", None, "blk"),
            P("expert", "blk", None),
        ),
        out_specs=P(("groups", "expert", "blk"), None),
        check_vma=False,
    )
```

time: 153 us -> 67.5 us (0.44)
  Pallas kernels: 0 us -> 63 us
  blocking collectives: 49.9 us -> 0 us
  waiting for transfers between devices: 47.3 us -> 0 us
  matrix products: 27.7 us -> 0 us
  between operations: 14.2 us -> 0.01 us
  starting transfers between devices: 5.05 us -> 0 us
  local copies, waits for them, and re-layouts: 6.29 us -> 1.69 us
    pallas_call x0 -> x1, Pallas kernels: none -> 63 us  [on_device(): pl.pallas_call(functools.partial(kernel, n), out_shape=jax.ShapeDtypeStru...]
    all_gather x1 -> x0, waiting for transfers between devices: 46.1 us -> none  [on_device(): piece = lax.all_gather(arrived, 'blk', axis=0, tiled=True)]
    unnamed x1 -> x0, blocking collectives: 36.1 us -> none
    dot_general x6 -> x0, matrix products: 27.7 us -> none  [the longest x1 13.5 us: on_device(): jnp.dot(ordered, down_local, preferred_element_type=jnp.float32)]
    all_to_all x2 -> x0, blocking collectives: 13.8 us -> none  [the longest x1 9.52 us: on_device(): lax.all_to_all(outputs, 'expert', split_axis=0, concat_axis=0, tiled=True)]
    unnamed x2 -> x0, starting transfers between devices: 5.04 us -> none
    reshape x4 -> x0, local copies, waits for them, and re-layouts: 4.2 us -> none  [the longest x1 1.59 us: on_device(): flat_rows = piece.reshape(-1, D)]
  transfers between devices with their start and end apart: 3 -> 0, of which waited for: 2 -> 0; matrix products, arithmetic and copies ran while one was open for 0% -> 0% of each run, Pallas kernels for 0% -> 0%
where the time goes in v1:
time: 67.5 us; the launch traced here: 67.3 us
  Pallas kernels  63 us (93%)
  other arithmetic  2.62 us (4%)
  local copies, waits for them, and re-layouts  1.69 us (3%)
    pallas_call x1, Pallas kernels, on_device(): pl.pallas_call(functools.partial(kernel, n), out_shape=jax.ShapeDtypeStru...  63 us
    unnamed x1, local copies, waits for them, and re-layouts  1.69 us

profile of v1, /device:TPU:1, one launch (start us, length us, event | category | flops | bytes accessed | tf_op | source)
XLA Modules:
  0.0 67.3 jit_solution(12014608453872661411)
XLA Ops:
  0.0 0.7 convert_bitcast_fusion.1
  0.7 0.7 %convert_bitcast_fusion = f32[2,20]{1,0:T(2,128)S(1)} fusion(s32[20,2]{0,1:T(2,128)} %param.17), kind=kLoop, calls=%fused_computation.4 | loop fusion | flops 40 | bytes 320 | tf_op jit(solution)/shard_map/convert_element_type | solution.py:386
  1.3 1.3 %select_maximum_fusion.meta = f32[8,128]{1,0:T(8,128)} fusion(f32[1,20]{1,0:T(1,128)S(1)} %convert_bitcast_fusion.1, f32[2,20]{1,0:T(2,128)} %bitcast.7, f32[2,20]{1,0:T(2,128)S(1)} %convert_bitcast_fusion), kind=kLoop, calls=%fused_computation | loop fusion | flops 11264 | bytes 4496 | tf_op jit(solution)/shard_map/concatenate | solution.py:385
  2.6 63.0 %shard_map.109 = bf16[20,6144]{1,0:T(8,128)(2,1)} custom-call(bf16[20,6144]{1,0:T(8,128)(2,1)} %residual.1, bf16[20,6144]{1,0:T(8,128)(2,1)} %queries.1, f32[8,128]{1,0:T(8,128)} %select_maximum_fusion.meta, f32[1,6144]{1,0:T(1,128)} %bitcast.6, bf16[20,32,1024]{2,1,0:T(8,128)(2,1)} %keys.1, bf16[20,32,1024]{2,1,0:T(8,128)(2,1)} %values.1, ...), custom_call_target="tpu_custom_call" | custom-call | tf_op jit(solution)/shard_map/pallas_call | solution.py:395
  65.6 1.7 %copy.13 = bf16[20,6144]{1,0:T(8,128)(2,1)} copy(bf16[20,6144]{1,0:T(8,128)(2,1)} %shard_map.109) | data formatting | bytes 491520

commit v2 on v1

--- a/solution.py
+++ b/solution.py
@@ -27,8 +27,8 @@
 
 
 def kernel(
-    n, residual, queries, meta, gain, keys, values, w_gate, w_up, w_down, mixed,
-    kbuf, vbuf, wg, wu, wd, qs, hid, live,
+    n, residual, queries, routes, scores_in, lengths_in, gain, keys, values, w_gate, w_up, w_down, mixed,
+    kbuf, vbuf, wg, wu, wd, qs, hid, live, meta, sc, pr,
     osend, inbox, gath, xfull, gacc, uacc, act,
     part, ybuf, red, zbuf, fin, pfin,
     kv_sem, wg_sem, wu_sem, wd_sem,
@@ -90,6 +90,10 @@
     def as_column(row):
         return jnp.sum(jnp.where(row_id == lane_id, row, 0.0), axis=1, keepdims=True)
 
+    meta[...] = jnp.full(meta.shape, -1.0, jnp.float32)
+    meta[0:2, 0:rows] = routes[...].astype(jnp.float32)
+    meta[2:4, 0:rows] = scores_in[...]
+    meta[4:5, 0:rows] = lengths_in[...].astype(jnp.float32)
     first, second = meta[0:1, :], meta[1:2, :]
     score0, score1 = meta[2:3, :], meta[3:4, :]
     lengths = as_column(meta[4:5, :])
@@ -145,30 +149,55 @@
     key_copy.wait()
     value_copy.wait()
 
-    def head(g, squares):
-        def cols(j):
-            return pl.ds(pl.multiple_of((g * GROUP + j) * HEAD_DIM, HEAD_DIM), HEAD_DIM)
-
-        kv_cols = pl.ds(pl.multiple_of(g * HEAD_DIM, HEAD_DIM), HEAD_DIM)
-        q = jnp.concatenate([qs[:, cols(j)] for j in range(GROUP)], axis=0).astype(jnp.bfloat16)
-        k = kbuf[:, :, kv_cols].reshape(rows * cache_len, HEAD_DIM)
-        v = vbuf[:, :, kv_cols].reshape(rows * cache_len, HEAD_DIM)
-        scores = lax.dot_general(
-            q, k, (((1,), (1,)), ((), ())), preferred_element_type=jnp.float32
-        ) * HEAD_DIM ** (-0.5)
-        scores = scores.reshape(GROUP, PAD, rows * cache_len)
-        scores = jnp.where(live[...][None] > 0, scores, -1e30)
-        exponent = jnp.exp(scores - jnp.max(scores, axis=-1, keepdims=True))
-        probs = exponent / jnp.sum(exponent, axis=-1, keepdims=True)
-        probs = probs.reshape(GROUP * PAD, rows * cache_len).astype(jnp.bfloat16)
-        attended = f32_dot(probs, v)
-        for j in range(GROUP):
-            h = hid[:, cols(j)] + attended[j * PAD:(j + 1) * PAD]
-            hid[:, cols(j)] = h
-            squares = squares + h * h
-        return squares
-
-    squares = lax.fori_loop(0, KV_HEADS, head, jnp.zeros((PAD, HEAD_DIM), jnp.float32))
+    batches = [(start, min(8, rows - start)) for start in range(0, rows, 8)]
+
+    def key_products(g, _):
+        for start, held in batches:
+            span = slice(start * cache_len, (start + held) * cache_len)
+            q = jnp.concatenate([qs[start:start + 8, head_cols(g, j)] for j in range(GROUP)], axis=0)
+            k = kbuf[start:start + held, :, kv_cols(g)].reshape(held * cache_len, HEAD_DIM)
+            sc[g, :, span] = lax.dot_general(
+                q.astype(jnp.bfloat16), k, (((1,), (1,)), ((), ())),
+                preferred_element_type=jnp.float32,
+            ) * HEAD_DIM ** (-0.5)
+        return _
+
+    def head_cols(g, j):
+        return pl.ds(pl.multiple_of((g * GROUP + j) * HEAD_DIM, HEAD_DIM), HEAD_DIM)
+
+    def kv_cols(g):
+        return pl.ds(pl.multiple_of(g * HEAD_DIM, HEAD_DIM), HEAD_DIM)
+
+    def softmax(g, _):
+        for start, held in batches:
+            span = slice(start * cache_len, (start + held) * cache_len)
+            scores = sc[g, :, span].reshape(GROUP, 8, held * cache_len)
+            scores = jnp.where(live[start:start + 8, span][None] > 0, scores, -1e30)
+            exponent = jnp.exp(scores - jnp.max(scores, axis=-1, keepdims=True))
+            probs = exponent * (1.0 / jnp.sum(exponent, axis=-1, keepdims=True))
+            pr[g, :, span] = probs.reshape(GROUP * 8, held * cache_len).astype(jnp.bfloat16)
+        return _
+
+    def value_products(g, squares):
+        sums = []
+        for (start, held), square in zip(batches, squares):
+            span = slice(start * cache_len, (start + held) * cache_len)
+            v = vbuf[start:start + held, :, kv_cols(g)].reshape(held * cache_len, HEAD_DIM)
+            attended = f32_dot(pr[g, :, span], v)
+            for j in range(GROUP):
+                h = hid[start:start + 8, head_cols(g, j)] + attended[j * 8:(j + 1) * 8]
+                hid[start:start + 8, head_cols(g, j)] = h
+                square = square + h * h
+            sums.append(square)
+        return tuple(sums)
+
+    lax.fori_loop(0, KV_HEADS, key_products, 0, unroll=8)
+    lax.fori_loop(0, KV_HEADS, softmax, 0, unroll=8)
+    squares = lax.fori_loop(
+        0, KV_HEADS, value_products,
+        tuple(jnp.zeros((8, HEAD_DIM), jnp.float32) for _ in batches), unroll=8,
+    )
+    squares = jnp.concatenate(squares, axis=0)
     inverse = lax.rsqrt(jnp.sum(squares, axis=1, keepdims=True) * (1.0 / width) + 1e-5)
 
     def in_chip(c):
@@ -191,10 +220,10 @@
             device_id={"blk": column_peer(k)}, device_id_type=MESH,
         )
 
-    def to_partner(c, y):
-        column = gath.at[c, y]
-        return pltpu.make_async_remote_copy(
-            column, column, y_sems.at[0, c], y_sems.at[1, c],
+    def to_partner(c, y, k):
+        piece = gath.at[c, y, lax.rem(zc + nc - k, nc)]
+        return pltpu.make_async_remote_copy(
+            piece, piece, y_sems.at[0, c, k], y_sems.at[1, c, k],
             device_id={"blk": y_partner}, device_id_type=MESH,
         )
 
@@ -221,6 +250,7 @@
         ).astype(jnp.bfloat16)
         for k in range(1, nc):
             along_column(c, k).start()
+        to_partner(c, yc, 0).start()
 
     span_a = lax.broadcasted_iota(jnp.int32, (TILE, TILE), 0)
     span_b = lax.broadcasted_iota(jnp.int32, (TILE, TILE), 1)
@@ -249,12 +279,13 @@
         def _():
             for k in range(1, nc):
                 from_column(s, k).wait_recv()
-            to_partner(s, yc).start()
+                to_partner(s, yc, k).start()
 
         @pl.when(s > 0)
         def _():
             c = s - 1
-            to_partner(c, 1 - yc).wait_recv()
+            for k in range(nc):
+                to_partner(c, 1 - yc, k).wait_recv()
             packed = gath[c].reshape(total, PACK)
             xfull[:, :PACK] = packed
             for group in groups:
@@ -278,9 +309,10 @@
         g = gacc[:, tile]
         act[:, tile] = (g / (1.0 + jnp.exp(-g)) * uacc[:, tile]).astype(jnp.bfloat16)
 
-    def sum_partner(c):
-        return pltpu.make_async_remote_copy(
-            part.at[c, 1 - yc], ybuf.at[c], ry_sems.at[0, c], ry_sems.at[1, c],
+    def sum_partner(c, k):
+        z = lax.rem(zc + k, nc)
+        return pltpu.make_async_remote_copy(
+            part.at[c, 1 - yc, z], ybuf.at[c, z], ry_sems.at[0, c, k], ry_sems.at[1, c, k],
             device_id={"blk": y_partner}, device_id_type=MESH,
         )
 
@@ -314,17 +346,20 @@
                 part[s, :, :, :, i * QUARTER:(i + 1) * QUARTER] = packed.reshape(
                     2, nc, PIECE, QUARTER
                 )
-            sum_partner(s).start()
+            for k in (*range(1, nc), 0):
+                sum_partner(s, k).start()
 
         @pl.when((s >= 1) & (s <= chunks))
         def _():
             c = s - 1
-            sum_partner(c).wait_recv()
-            red[c] = (
-                part[c, yc].astype(jnp.float32) + ybuf[c].astype(jnp.float32)
-            ).astype(jnp.bfloat16)
-            for k in range(1, nc):
-                sum_column(c, k).start()
+            for k in (*range(1, nc), 0):
+                sum_partner(c, k).wait_recv()
+                z = lax.rem(zc + k, nc)
+                red[c, z] = (
+                    part[c, yc, z].astype(jnp.float32) + ybuf[c, z].astype(jnp.float32)
+                ).astype(jnp.bfloat16)
+                if k > 0:
+                    sum_column(c, k).start()
 
         @pl.when((s >= 2) & (s <= chunks + 1))
         def _():
@@ -363,9 +398,10 @@
     @pl.loop(0, chunks)
     def _(c):
         in_chip(c).wait_send()
-        to_partner(c, yc).wait_send()
-        sum_partner(c).wait_send()
         swap(c).wait_send()
+        for k in range(nc):
+            to_partner(c, yc, k).wait_send()
+            sum_partner(c, k).wait_send()
         for k in range(1, nc):
             along_column(c, k).wait_send()
             sum_column(c, k).wait_send()
@@ -381,13 +417,6 @@
     units = w_gate.shape[2]
     chunks = width // CHUNK
     total = n * PIECE
-    meta = jnp.pad(
-        jnp.concatenate(
-            [routes.T.astype(jnp.float32), gate_scores.T, lengths[None].astype(jnp.float32)], axis=0
-        ),
-        ((0, 3), (0, TILE - rows)),
-        constant_values=-1.0,
-    )
     bf16, f32 = jnp.bfloat16, jnp.float32
     vmem = pl.BlockSpec(memory_space=pltpu.VMEM)
     anywhere = pl.BlockSpec(memory_space=pl.ANY)
@@ -395,7 +424,7 @@
     return pl.pallas_call(
         functools.partial(kernel, n),
         out_shape=jax.ShapeDtypeStruct((rows, width), bf16),
-        in_specs=[vmem] * 4 + [anywhere] * 5,
+        in_specs=[vmem] * 6 + [anywhere] * 5,
         out_specs=vmem,
         scratch_shapes=[
             pltpu.VMEM(keys.shape, bf16),
@@ -406,6 +435,9 @@
             pltpu.VMEM((PAD, width), f32),
             pltpu.VMEM((PAD, width), f32),
             pltpu.VMEM((PAD, rows * cache_len), f32),
+            pltpu.VMEM((8, TILE), f32),
+            pltpu.VMEM((KV_HEADS, GROUP * 8, rows * cache_len), f32),
+            pltpu.VMEM((KV_HEADS, GROUP * 8, rows * cache_len), bf16),
             pltpu.VMEM((chunks, PIECE, PACK), bf16),
             pltpu.VMEM((chunks, PIECE, PACK), bf16),
             pltpu.VMEM((chunks, 2, nc, PIECE, PACK), bf16),
@@ -425,15 +457,18 @@
             dma((chunks,)),
             dma((2, chunks)),
             dma((2, chunks, nc - 1)),
-            dma((2, chunks)),
-            dma((2, chunks)),
+            dma((2, chunks, nc)),
+            dma((2, chunks, nc)),
             dma((2, chunks, nc - 1)),
             dma((2, chunks)),
         ],
         compiler_params=pltpu.CompilerParams(
             collective_id=0, has_side_effects=True, vmem_limit_bytes=60 * 1024 * 1024
         ),
-    )(residual, queries, meta, norm_gain.reshape(1, width), keys, values, w_gate, w_up, w_down)
+    )(
+        residual, queries, routes.T, gate_scores.T, lengths.reshape(1, rows),
+        norm_gain.reshape(1, width), keys, values, w_gate, w_up, w_down,
+    )
 
 
 def solution(mesh):

time: 67.5 us -> 57.6 us (0.85)
  Pallas kernels: 63 us -> 55.7 us
  other arithmetic: 2.62 us -> 0 us
    pallas_call x1, Pallas kernels: 63 us -> 55.7 us  [on_device(): pl.pallas_call(functools.partial(kernel, n), out_shape=jax.ShapeDtypeStru...]
    convert_element_type x2 -> x0, other arithmetic: 1.34 us -> none  [the longest x1 0.68 us: on_device(): routes.T.astype(jnp.float32)]
    concatenate x1 -> x0, other arithmetic: 1.28 us -> none  [on_device(): jnp.concatenate([routes.T.astype(jnp.float32), gate_scores.T, lengths[Non...]
where the time goes in v2:
time: 57.6 us; the launch traced here: 57.4 us
  Pallas kernels  55.7 us (97%)
  local copies, waits for them, and re-layouts  1.69 us (3%)
    pallas_call x1, Pallas kernels, on_device(): pl.pallas_call(functools.partial(kernel, n), out_shape=jax.ShapeDtypeStru...  55.7 us
    unnamed x1, local copies, waits for them, and re-layouts  1.69 us

profile of v2, /device:TPU:1, one launch (start us, length us, event | category | flops | bytes accessed | tf_op | source)
XLA Modules:
  0.0 57.4 jit_solution(14009665043608167627)
XLA Ops:
  0.0 55.7 %shard_map.109 = bf16[20,6144]{1,0:T(8,128)(2,1)} custom-call(bf16[20,6144]{1,0:T(8,128)(2,1)} %residual.1, bf16[20,6144]{1,0:T(8,128)(2,1)} %queries.1, s32[2,20]{1,0:T(2,128)} %bitcast.5, f32[2,20]{1,0:T(2,128)} %bitcast.6, s32[1,20]{1,0:T(1,128)} %bitcast.7, f32[1,6144]{1,0:T(1,128)} %bitcast.4, bf16[20,32,1024]{2,1,0:T(8,128)(2,1)} %keys.1, ...), custom_call_target="tpu_custom_call" | custom-call | tf_op jit(solution)/shard_map/pallas_call | solution.py:424
  55.8 1.7 %copy.13 = bf16[20,6144]{1,0:T(8,128)(2,1)} copy(bf16[20,6144]{1,0:T(8,128)(2,1)} %shard_map.109) | data formatting | bytes 491520
